TPU v7x, 512 devices: a whole 4x8x8 slice. The times are simulated.
512 devices in a mesh: pair: 256 (over z, y, x), tm: 2 (over core).
Axes of the slice: x: 4, y: 8, z: 8, core: 2. Of those that a mesh axis runs over, the one named last changes fastest.
Arguments:
- traces: float32 [8192, 2, 4096], P('pair', 'tm'), may hold values from -600 to 600, as said below
- pair_list: int32 [8192, 2], P('pair'), may hold values from 0 to 8191, as said below
- live_pairs: int32 [256], P('pair'), may hold values from 4 to 32, as said below
Outputs:
- correlations: float32 [8192, 2048], P(('pair', 'tm'))
Inputs may be any that keep to these rules, and one draw needn't show every extreme that they name: `pair_list`: rows j * 32 to (j + 1) * 32 - 1 have their first channel in [j * 32, (j + 1) * 32); the second channel differs from the first by at most 32, and by exactly 32 in some row of every draw. The first live_pairs[j] slots of owner j are live; some owner has all 32 live. `traces`: records in arbitrary units.
All inputs are finite; a program needn't handle non-finite values.
Results may differ from a plain program's by a relative error of at most 0.0085.
Values may be sent and summed in bfloat16 or wider, within the bound.
A program may use at most 64 MiB of HBM per device.

v0:
```python
import math

import jax
import jax.numpy as jnp
from jax import lax
from jax.sharding import PartitionSpec as P

RADIX = 64
NT = 4096
FB = 2048
NLAG = 2048
HALF = 64


TWO_PI = 2.0 * math.pi
EPSILON = 1e-06
HIGHEST = lax.Precision.HIGHEST


def extended_2(cells, sides, width):
    for axis, dim in sides:
        count = lax.axis_size(axis)
        ends = count - 1
        head = lax.slice_in_dim(cells, 0, width, axis=dim)
        tail = lax.slice_in_dim(cells, cells.shape[dim] - width, cells.shape[dim], axis=dim)
        cells = jnp.concatenate(
            [
                lax.ppermute(tail, axis, [(i, (i + 1) % count) for i in range(ends)]),
                cells,
                lax.ppermute(head, axis, [((i + 1) % count, i) for i in range(ends)]),
            ],
            axis=dim,
        )
    return cells


def radix_tables():
    indices = jnp.arange(RADIX)
    product = indices[:, None] * indices[None, :] % RADIX
    angles = TWO_PI * product.astype(jnp.float32) / RADIX
    twist = TWO_PI * (indices[:, None] * indices[None, :]).astype(jnp.float32) / NT
    return (jnp.cos(angles), jnp.sin(angles), jnp.cos(twist), jnp.sin(twist))


def forward_bins(traces):
    channels, segments = (traces.shape[0], traces.shape[1])
    cosine, sine, twist_cos, twist_sin = radix_tables()
    blocks = traces.reshape(channels, segments, RADIX, RADIX)
    section_real = jnp.einsum("kn,csnm->cskm", cosine, blocks, precision=HIGHEST)
    section_imag = -jnp.einsum("kn,csnm->cskm", sine, blocks, precision=HIGHEST)
    turned_real = section_real * twist_cos + section_imag * twist_sin
    turned_imag = section_imag * twist_cos - section_real * twist_sin
    final_real = jnp.einsum("cskm,jm->csjk", turned_real, cosine, precision=HIGHEST) + jnp.einsum(
        "cskm,jm->csjk", turned_imag, sine, precision=HIGHEST
    )
    final_imag = jnp.einsum("cskm,jm->csjk", turned_imag, cosine, precision=HIGHEST) - jnp.einsum(
        "cskm,jm->csjk", turned_real, sine, precision=HIGHEST
    )
    final_real = final_real.reshape(channels, segments, NT)[..., 1 : FB + 1]
    final_imag = final_imag.reshape(channels, segments, NT)[..., 1 : FB + 1]
    return (final_real, final_imag)


def whiten(traces):
    real_part, imag_part = forward_bins(traces)
    magnitude = jnp.sqrt(real_part * real_part + imag_part * imag_part)
    block_width = min(256, FB)
    window_len = block_width + 2 * HALF
    padded = jnp.pad(magnitude, ((0, 0), (0, 0), (HALF, HALF)))
    inputs = jnp.arange(window_len)[:, None]
    outputs = jnp.arange(block_width)[None, :]
    banded = ((inputs >= outputs) & (inputs <= outputs + 2 * HALF)).astype(jnp.float32)
    partial_sums = [
        jnp.einsum(
            "csi,io->cso",
            padded[:, :, block_start : block_start + window_len],
            banded,
            precision=HIGHEST,
        )
        for block_start in range(0, FB, block_width)
    ]
    window_sum = jnp.concatenate(partial_sums, axis=-1)
    centre = jnp.arange(FB)
    counted = jnp.minimum(centre + HALF, FB - 1) - jnp.maximum(centre - HALF, 0) + 1
    level_mean = window_sum / counted.astype(jnp.float32)
    inverse = 1.0 / (level_mean + EPSILON)
    return jnp.concatenate([real_part * inverse, imag_part * inverse], axis=-1).astype(jnp.bfloat16)


def lag_rows(rows, scale):
    row_count = rows.shape[0]
    cosine, sine, twist_cos, twist_sin = radix_tables()
    zero_col = jnp.zeros((row_count, 1), jnp.float32)
    tail = jnp.zeros((row_count, NT - FB - 1), jnp.float32)
    full_real = jnp.concatenate([zero_col, rows[:, :FB], tail], axis=1).reshape(
        row_count, RADIX, RADIX
    )
    full_imag = jnp.concatenate([zero_col, rows[:, FB:], tail], axis=1).reshape(
        row_count, RADIX, RADIX
    )
    section_real = jnp.einsum("rab,an->rbn", full_real, cosine, precision=HIGHEST) - jnp.einsum(
        "rab,an->rbn", full_imag, sine, precision=HIGHEST
    )
    section_imag = jnp.einsum("rab,an->rbn", full_imag, cosine, precision=HIGHEST) + jnp.einsum(
        "rab,an->rbn", full_real, sine, precision=HIGHEST
    )
    turned_real = section_real * twist_cos - section_imag * twist_sin
    turned_imag = section_imag * twist_cos + section_real * twist_sin
    signal = jnp.einsum("rbn,bp->rpn", turned_real, cosine, precision=HIGHEST) - jnp.einsum(
        "rbn,bp->rpn", turned_imag, sine, precision=HIGHEST
    )
    signal = signal.reshape(row_count, NT) * scale
    return jnp.concatenate([signal[:, NT - NLAG // 2 :], signal[:, : NLAG // 2]], axis=1)


def inverse_rows(cross_spec, live_count, segment_total):
    row_total = cross_spec.shape[0]
    scale = 1.0 / math.sqrt(FB * segment_total)
    slot_index = jnp.arange(row_total)
    product = lag_rows(cross_spec, scale)
    return jnp.where((slot_index < live_count)[:, None], product, 0.0)


def shards(traces, pair_list, live_pairs):
    whitened = whiten(traces)
    own_channels = whitened.shape[0]
    extended = extended_2(whitened, (("pair", 0),), own_channels)
    anchor = lax.axis_index("pair") * own_channels - own_channels
    first_rows = jnp.take(extended, pair_list[:, 0] - anchor, axis=0).astype(jnp.float32)
    second_rows = jnp.take(extended, pair_list[:, 1] - anchor, axis=0).astype(jnp.float32)
    real_a, imag_a = (first_rows[..., :FB], first_rows[..., FB:])
    real_b, imag_b = (second_rows[..., :FB], second_rows[..., FB:])
    cross_real = jnp.sum(real_a * real_b + imag_a * imag_b, axis=1)
    cross_imag = jnp.sum(imag_a * real_b - real_a * imag_b, axis=1)
    cross_spec = jnp.concatenate([cross_real, cross_imag], axis=-1)
    segment_total = traces.shape[1] * lax.axis_size("tm")
    live_count = live_pairs[0]
    partial_lags = inverse_rows(cross_spec, live_count, segment_total)
    return lax.psum_scatter(partial_lags, "tm", scatter_dimension=0, tiled=True)


def solution(mesh):
    placed = (P("pair", "tm", None), P("pair", None), P("pair"))
    return jax.shard_map(
        shards, mesh=mesh, in_specs=placed, out_specs=P(("pair", "tm"), None), check_vma=False
    )
```

profile of v0, /device:TPU:1, one launch (start us, length us, event | category | flops | bytes accessed | tf_op | source)
XLA Modules:
  0.0 94.6 jit_solution(706433268573508466)
XLA Ops:
  6.5 0.1 fusion.63
  6.7 0.1 fusion.62
  6.8 2.3 %reduce = f32[32,4096]{1,0:T(8,128)S(1)} reduce(f32[32,1,4096]{2,1,0:T(1,128)} %param.5, f32[]{:T(128)} %constant.74), dimensions={1}, to_apply=%param.5.reduce_sub_computation | reduce | bytes 1048580 | tf_op args[0]
  9.1 0.4 reshape.370
  9.5 1.2 %convolution_bitcast_fusion = f32[32,1,64,64]{3,2,0,1:T(8,128)S(1)} fusion(f32[32,64,64]{2,1,0:T(8,128)S(1)} %reshape.370), kind=kOutput, calls=%fused_computation.13 | convolution fusion | flops 100720640 | bytes 1048576 | tf_op jit(solution)/shard_map/kn,csnm->cskm/dot_general | solution.py:49
  10.7 1.2 %fusion.4 = f32[32,1,64,64]{3,2,0,1:T(8,128)S(1)} fusion(f32[32,64,64]{2,1,0:T(8,128)S(1)} %reshape.370), kind=kOutput, calls=%fused_computation.12 | convolution fusion | flops 100851712 | bytes 1048576 | tf_op jit(solution)/shard_map/kn,csnm->cskm/dot_general | solution.py:50
  11.8 0.1 copy.19
  11.9 0.1 copy.21
  12.0 3.3 %fusion.13 = f32[64,32,64]{2,0,1:T(8,128)S(1)} fusion(f32[32,1,64,64]{3,2,0,1:T(8,128)S(1)} %convolution_bitcast_fusion, f32[32,1,64,64]{3,2,0,1:T(8,128)S(1)} %fusion.4, f32[64,64]{1,0:T(8,128)S(1)} %copy.21, f32[64,64]{1,0:T(8,128)S(1)} %copy.19), kind=kOutput, calls=%fused_computation.30 | convolution fusion | flops 101113856 | bytes 1605632 | tf_op jit(solution)/shard_map/cskm,jm->csjk/dot_general | solution.py:56
  15.3 3.3 %fusion.17 = f32[64,32,64]{2,0,1:T(8,128)S(1)} fusion(f32[32,1,64,64]{3,2,0,1:T(8,128)S(1)} %fusion.4, f32[32,1,64,64]{3,2,0,1:T(8,128)S(1)} %convolution_bitcast_fusion, f32[64,64]{1,0:T(8,128)S(1)} %copy.21, f32[64,64]{1,0:T(8,128)S(1)} %copy.19), kind=kOutput, calls=%fused_computation.34 | convolution fusion | flops 101113856 | bytes 1605632 | tf_op jit(solution)/shard_map/cskm,jm->csjk/dot_general | solution.py:53
  18.6 4.3 %fusion.2 = f32[32,1,64,64]{3,2,0,1:T(8,128)} fusion(f32[64,32,64]{2,0,1:T(8,128)S(1)} %fusion.13, f32[32,1,64,64]{3,2,0,1:T(8,128)S(1)} %fusion.4, f32[32,1,64,64]{3,2,0,1:T(8,128)S(1)} %convolution_bitcast_fusion, f32[64,64]{1,0:T(8,128)S(1)} %copy.21, f32[64,64]{1,0:T(8,128)S(1)} %copy.19), kind=kOutput, calls=%fused_computation.8 | convolution fusion | flops 101244928 | bytes 2129920 | tf_op jit(solution)/shard_map/cskm,jm->csjk/dot_general | solution.py:56
  22.9 2.4 %reshape.374 = f32[32,1,4096]{2,0,1:T(8,128)} reshape(f32[32,1,64,64]{3,2,0,1:T(8,128)} %fusion.2) | data formatting | bytes 1048576 | tf_op jit(solution)/shard_map/reshape | solution.py:60
  25.2 4.4 %fusion.3 = f32[32,1,64,64]{3,2,0,1:T(8,128)} fusion(f32[64,32,64]{2,0,1:T(8,128)S(1)} %fusion.17, f32[32,1,64,64]{3,2,0,1:T(8,128)S(1)} %convolution_bitcast_fusion, f32[32,1,64,64]{3,2,0,1:T(8,128)S(1)} %fusion.4, f32[64,64]{1,0:T(8,128)S(1)} %copy.21, f32[64,64]{1,0:T(8,128)S(1)} %copy.19), kind=kOutput, calls=%fused_computation.10 | convolution fusion | flops 101244928 | bytes 2129920 | tf_op jit(solution)/shard_map/cskm,jm->csjk/dot_general | solution.py:53
  29.7 1.6 %reshape.373 = f32[32,1,4096]{2,0,1:T(8,128)S(1)} reshape(f32[32,1,64,64]{3,2,0,1:T(8,128)} %fusion.3) | data formatting | bytes 1048576 | tf_op jit(solution)/shard_map/reshape | solution.py:59
  31.3 0.2 add_sqrt_fusion
  31.5 0.3 fusion.12
  31.8 0.3 fusion.11
  32.1 0.3 fusion.10
  32.3 0.3 fusion.9
  32.6 0.3 fusion.8
  32.9 0.3 fusion.7
  33.2 0.0 copy-start.1
  33.2 0.3 fusion.6
  33.4 0.3 fusion.5
  33.7 0.2 multiply_convert_fusion.1
  34.0 4.0 %collective-permute-start = (bf16[32,1,4096]{2,0,1:T(8,128)(2,1)S(1)}, bf16[32,1,4096]{2,0,1:T(8,128)(2,1)S(1)}, u32[]{:S(2)}, u32[]{:S(2)}) collective-permute-start(bf16[32,1,4096]{2,0,1:T(8,128)(2,1)S(1)} %pad_maximum_fusion), channel_id=1, source_target_pairs={{0,2},{2,4},{4,6},{6,8},{8,10},{10,12},{12,14},{14,16},{16,18},{18... | collective-permute-start | bytes 786440 | tf_op jit(solution)/shard_map/ppermute | solution.py:28
  37.9 1.3 %collective-permute-start.1 = (bf16[32,1,4096]{2,0,1:T(8,128)(2,1)S(1)}, bf16[32,1,4096]{2,0,1:T(8,128)(2,1)S(1)}, u32[]{:S(2)}, u32[]{:S(2)}) collective-permute-start(bf16[32,1,4096]{2,0,1:T(8,128)(2,1)S(1)} %pad_maximum_fusion), channel_id=1, source_target_pairs={{2,0},{4,2},{6,4},{8,6},{10,8},{12,10},{14,12},{16,14},{18,16},{20... | collective-permute-start | bytes 786440 | tf_op jit(solution)/shard_map/ppermute | solution.py:30
  39.9 1.3 %collective-permute-done = bf16[32,1,4096]{2,0,1:T(8,128)(2,1)S(1)} collective-permute-done((bf16[32,1,4096]{2,0,1:T(8,128)(2,1)S(1)}, bf16[32,1,4096]{2,0,1:T(8,128)(2,1)S(1)}, u32[]{:S(2)}, u32[]{:S(2)}) %collective-permute-start) | collective-permute-done | bytes 262176 | tf_op jit(solution)/shard_map/ppermute | solution.py:28
  41.2 3.8 %collective-permute-done.1 = bf16[32,1,4096]{2,0,1:T(8,128)(2,1)S(1)} collective-permute-done((bf16[32,1,4096]{2,0,1:T(8,128)(2,1)S(1)}, bf16[32,1,4096]{2,0,1:T(8,128)(2,1)S(1)}, u32[]{:S(2)}, u32[]{:S(2)}) %collective-permute-start.1) | collective-permute-done | bytes 262176 | tf_op jit(solution)/shard_map/ppermute | solution.py:30
  45.0 0.1 maximum_bitcast_fusion
  45.1 0.7 gather_fusion
  45.8 0.7 gather_fusion.1
  46.5 0.1 fusion.31
  46.7 0.1 add_bitcast_fusion
  46.8 0.3 concatenate.62
  47.1 0.4 reshape.383
  47.5 1.8 %fusion.56 = f32[32,64,64]{2,1,0:T(8,128)S(1)} fusion(f32[32,64,64]{2,1,0:T(8,128)S(1)} %reshape.383), kind=kOutput, calls=%fused_computation.89 | convolution fusion | flops 100720640 | bytes 1048576 | tf_op jit(solution)/shard_map/rab,an->rbn/dot_general | solution.py:101
  49.3 1.0 %concatenate.63 = f32[32,4096]{1,0:T(8,128)} concatenate(f32[32,1]{1,0:T(8,128)S(1)} %broadcast_in_dim.22, f32[32,2048]{1,0:T(8,128)S(1)} %get-tuple-element.11, f32[32,2047]{1,0:T(8,128)S(1)} %broadcast_in_dim.23), dimensions={1} | concatenate | bytes 1048576 | tf_op jit(solution)/shard_map/concatenate | solution.py:98
  50.3 1.5 %reshape.384 = f32[32,64,64]{2,1,0:T(8,128)S(1)} reshape(f32[32,4096]{1,0:T(8,128)} %concatenate.63) | data formatting | bytes 1048576 | tf_op jit(solution)/shard_map/reshape | solution.py:98
  51.8 1.8 %fusion.54 = f32[32,64,64]{2,1,0:T(8,128)S(1)} fusion(f32[32,64,64]{2,1,0:T(8,128)S(1)} %reshape.384), kind=kOutput, calls=%fused_computation.87 | convolution fusion | flops 100720640 | bytes 1048576 | tf_op jit(solution)/shard_map/rab,an->rbn/dot_general | solution.py:104
  53.6 1.8 %convolution_subtract_fusion.1 = f32[32,64,64]{2,1,0:T(8,128)S(1)} fusion(f32[32,64,64]{2,1,0:T(8,128)S(1)} %fusion.56, f32[32,64,64]{2,1,0:T(8,128)S(1)} %reshape.384), kind=kOutput, calls=%fused_computation.6 | convolution fusion | flops 100851712 | bytes 1572864 | tf_op jit(solution)/shard_map/rab,an->rbn/dot_general | solution.py:101
  55.5 1.8 %convolution_add_fusion = f32[32,64,64]{2,1,0:T(8,128)S(1)} fusion(f32[32,64,64]{2,1,0:T(8,128)S(1)} %fusion.54, f32[32,64,64]{2,1,0:T(8,128)S(1)} %reshape.383), kind=kOutput, calls=%fused_computation.5 | convolution fusion | flops 100851712 | bytes 1572864 | tf_op jit(solution)/shard_map/rab,an->rbn/dot_general | solution.py:104
  57.3 1.2 %fusion.22 = f32[64,32,64]{2,0,1:T(8,128)S(1)} fusion(f32[32,64,64]{2,1,0:T(8,128)S(1)} %convolution_add_fusion, f32[32,64,64]{2,1,0:T(8,128)S(1)} %convolution_subtract_fusion.1, f32[64,64]{1,0:T(8,128)S(1)} %copy.21, f32[64,64]{1,0:T(8,128)S(1)} %copy.19), kind=kOutput, calls=%fused_computation.39 | convolution fusion | flops 101113856 | bytes 1605632 | tf_op jit(solution)/shard_map/rbn,bp->rpn/dot_general | solution.py:109
  58.5 1.2 %fusion.1 = f32[32,64,64]{2,1,0:T(8,128)S(1)} fusion(f32[64,32,64]{2,0,1:T(8,128)S(1)} %fusion.22, f32[32,64,64]{2,1,0:T(8,128)S(1)} %convolution_subtract_fusion.1, f32[32,64,64]{2,1,0:T(8,128)S(1)} %convolution_add_fusion, f32[64,64]{1,0:T(8,128)S(1)} %copy.21, f32[64,64]{1,0:T(8,128)S(1)} %copy.19), kind=kOutput, calls=%fused_computation.4 | convolution fusion | flops 101376000 | bytes 2129920 | tf_op jit(solution)/shard_map/rbn,bp->rpn/dot_general | solution.py:109
  59.6 0.4 mul.296
  60.0 0.8 maximum_select_fusion
  60.8 0.0 reduce-scatter.2.cloned.1.call-update
  60.8 26.9 %reduce-scatter.2.cloned.1.call-done = f32[16,2048]{1,0:T(8,128)} async-done(((f32[32,2048]{1,0:T(8,128)}), f32[16,2048]{1,0:T(8,128)}) %reduce-scatter.2.cloned.1.call-update) | async-done | bytes 131088 | tf_op jit(solution)/shard_map/reduce_scatter | solution.py:139
  (14 shorter events, 0.1 us)
Async XLA Ops:
  6.5 81.2 %reduce-scatter.2.cloned.1.call-start = ((), (), s32[]{:S(2)}) async-start(), calls=%async_computation.1 | async-start | bytes 393216 | tf_op jit(solution)/shard_map/reduce_scatter | solution.py:139
  29.7 1.6 %copy-start = (f32[32,1,4096]{2,0,1:T(8,128)S(1)}, f32[32,1,4096]{2,0,1:T(8,128)}, u32[]{:S(2)}) copy-start(f32[32,1,4096]{2,0,1:T(8,128)} %reshape.374) | copy-start | bytes 1572868
  33.2 6.7 %copy-start.1 = (s32[32,2]{0,1:T(2,128)S(1)}, s32[32,2]{0,1:T(2,128)}, u32[]{:S(2)}) copy-start(s32[32,2]{0,1:T(2,128)} %param.6) | copy-start | bytes 772
  34.0 7.3 %collective-permute-start = (bf16[32,1,4096]{2,0,1:T(8,128)(2,1)S(1)}, bf16[32,1,4096]{2,0,1:T(8,128)(2,1)S(1)}, u32[]{:S(2)}, u32[]{:S(2)}) collective-permute-start(bf16[32,1,4096]{2,0,1:T(8,128)(2,1)S(1)} %pad_maximum_fusion), channel_id=1, source_target_pairs={{0,2},{2,4},{4,6},{6,8},{8,10},{10,12},{12,14},{14,16},{16,18},{18... | collective-permute-start | bytes 786440 | tf_op jit(solution)/shard_map/ppermute | solution.py:28
  37.9 7.1 %collective-permute-start.1 = (bf16[32,1,4096]{2,0,1:T(8,128)(2,1)S(1)}, bf16[32,1,4096]{2,0,1:T(8,128)(2,1)S(1)}, u32[]{:S(2)}, u32[]{:S(2)}) collective-permute-start(bf16[32,1,4096]{2,0,1:T(8,128)(2,1)S(1)} %pad_maximum_fusion), channel_id=1, source_target_pairs={{2,0},{4,2},{6,4},{8,6},{10,8},{12,10},{14,12},{16,14},{18,16},{20... | collective-permute-start | bytes 786440 | tf_op jit(solution)/shard_map/ppermute | solution.py:30
Sparse Core Ops, SparseCore 0:
  61.0 26.7 reduce-scatter.1
where the time goes:
time: 94.9 us; the launch traced here: 94.6 us
  waiting for transfers between devices  32 us (34%)
  matrix products  29.4 us (31%)
  between operations  14.3 us (15%)
  local copies, waits for them, and re-layouts  9.56 us (10%)
  starting transfers between devices  5.26 us (6%)
  other arithmetic  4.07 us (4%)
    reduce_scatter x1, waiting for transfers between devices, shards(): return lax.psum_scatter(partial_lags, 'tm', scatter_dimension=0, tiled=True)  26.9 us
    dot_general x1, matrix products, forward_bins(): jnp.einsum('cskm,jm->csjk', turned_imag, sine, precision=HIGHEST)  4.42 us
    dot_general x1, matrix products, forward_bins(): jnp.einsum('cskm,jm->csjk', turned_real, sine, precision=HIGHEST)  4.26 us
    ppermute x1, starting transfers between devices, extended_2(): lax.ppermute(tail, axis, [(i, (i + 1) % count) for i in range(ends)])  3.96 us
    ppermute x1, waiting for transfers between devices, extended_2(): lax.ppermute(head, axis, [((i + 1) % count, i) for i in range(ends)])  3.83 us
    dot_general x1, matrix products, forward_bins(): jnp.einsum('cskm,jm->csjk', turned_imag, cosine, precision=HIGHEST)  3.3 us
    dot_general x1, matrix products, forward_bins(): jnp.einsum('cskm,jm->csjk', turned_real, cosine, precision=HIGHEST)  3.29 us
    reshape x1, local copies, waits for them, and re-layouts, forward_bins(): final_imag = final_imag.reshape(channels, segments, NT)[..., 1:FB + 1]  2.38 us
  transfers between devices with their start and end apart: 3, of which 3 were waited for; matrix products, arithmetic and copies ran while one was open for 0% of the time, Pallas kernels for 0%

commit v1 on v0

v1 whole, which is shorter than its diff:
```python
import functools
import math

import jax
import jax.numpy as jnp
import numpy as np
from jax import lax
from jax.experimental import pallas as pl
from jax.experimental.pallas import tpu as pltpu
from jax.sharding import PartitionSpec as P

NT = 4096
FB = 2048
NLAG = 2048
HALF = 64
EPSILON = 1e-06

RADIX = 32
LANES = 128
SLABS = 16
CHUNK = 8
MESH = pl.DeviceIdType.MESH


def split(table):
    high = table.astype(jnp.bfloat16)
    low = (table - high.astype(np.float64)).astype(jnp.bfloat16)
    return np.stack([high, low])


def tables():
    n0 = np.arange(LANES)
    k2 = np.arange(LANES // 2)
    q = np.concatenate([k2, LANES - 1 - k2])
    sign = np.concatenate([np.ones(LANES // 2), -np.ones(LANES // 2)])
    angle = 2.0 * math.pi * (n0[:, None] * q[None, :] % LANES) / LANES
    cos, sin = np.cos(angle), np.sin(angle)
    forward = np.block([[cos, -sin * sign], [sin, cos * sign]])
    inverse = np.block([[cos.T, sin.T], [-sin.T * sign[:, None], cos.T * sign[:, None]]])
    inverse = inverse / 64.0
    s = np.arange(SLABS + 1)
    twist = 2.0 * math.pi * (s[:, None] * n0[None, :]) / NT
    k1 = np.stack([np.where(s[:16] == 0, 16, s[:16]), 32 - s[:16]], axis=1)
    index = (k1[:, :, None] - 1 + RADIX * k2[None, None, :]).reshape(SLABS, LANES)
    counted = np.minimum(index + HALF, FB - 1) - np.maximum(index - HALF, 0) + 1
    small = np.zeros((56, LANES))
    small[0:17] = np.cos(twist)
    small[17:34] = np.sin(twist)
    small[34:50] = counted
    return split(forward), split(inverse), small.astype(np.float32)


def scaled(value, factor):
    return value if factor == 1.0 else -value if factor == -1.0 else value * factor


def real_dft(values):
    count = len(values)
    if count == 2:
        return [(values[0] + values[1], None), (values[0] - values[1], None)]
    even, odd = real_dft(values[0::2]), real_dft(values[1::2])
    quarter = count // 4
    bins = [None] * (count // 2 + 1)
    bins[0] = (even[0][0] + odd[0][0], None)
    bins[count // 2] = (even[0][0] - odd[0][0], None)
    for k in range(1, quarter):
        c, s = math.cos(2.0 * math.pi * k / count), math.sin(2.0 * math.pi * k / count)
        (er, ei), (pr, pi) = even[k], odd[k]
        if 8 * k == count:
            tr, ti = (pr + pi) * c, (pi - pr) * c
        else:
            tr, ti = pr * c + pi * s, pi * c - pr * s
        bins[k] = (er + tr, ei + ti)
        bins[count // 2 - k] = (er - tr, ti - ei)
    er, pr = even[quarter][0], odd[quarter][0]
    bins[quarter] = (er, -pr)
    return bins


def real_sum(bins, count, wanted):
    if count == 2:
        (ar, _), (br, _) = bins
        return {l: ar + br if l == 0 else ar - br for l in wanted}
    quarter = count // 4
    even, odd = [], []
    for s in range(quarter):
        (ar, ai), (br, bi) = bins[s], bins[count // 2 - s]
        if s == 0:
            even.append((ar + br, None))
            odd.append((ar - br, None))
            continue
        even.append((ar + br, ai - bi))
        dr, di = ar - br, ai + bi
        c, n = math.cos(2.0 * math.pi * s / count), math.sin(2.0 * math.pi * s / count)
        if 8 * s == count:
            odd.append(((dr - di) * c, (dr + di) * c))
        else:
            odd.append((dr * c - di * n, dr * n + di * c))
    mr, mi = bins[quarter]
    even.append((mr, None))
    odd.append((-mi, None))
    half = count // 2
    from_even = real_sum(even, half, sorted({l // 2 for l in wanted if l % 2 == 0}))
    from_odd = real_sum(odd, half, sorted({l // 2 for l in wanted if l % 2 == 1}))
    return {l: (from_odd if l % 2 else from_even)[l // 2] for l in wanted}


def halves(value):
    high = value.astype(jnp.bfloat16)
    return high, (value - high.astype(jnp.float32)).astype(jnp.bfloat16)


def dot3(value, table):
    high, low = halves(value)
    dot = functools.partial(jnp.dot, preferred_element_type=jnp.float32)
    return dot(high, table[0]) + (dot(low, table[0]) + dot(high, table[1]))


def spectra(x_ref, small, forward, base):
    values = [x_ref[pl.ds(base * RADIX + n1, CHUNK, stride=RADIX), :] for n1 in range(RADIX)]
    turned_re, turned_im = [], []
    for s, (re, im) in enumerate(real_dft(values)):
        c, n = small[s : s + 1, :], small[17 + s : 18 + s, :]
        if s == 0:
            turned_re.append(re)
            turned_im.append(jnp.zeros_like(re))
        elif im is None:
            turned_re.append(re * c)
            turned_im.append(-re * n)
        else:
            turned_re.append(re * c + im * n)
            turned_im.append(im * c - re * n)
    rows = jnp.concatenate(
        [jnp.concatenate(turned_re, axis=0), jnp.concatenate(turned_im, axis=0)], axis=1
    )
    final = dot3(rows, forward)
    re = [final[s * CHUNK : (s + 1) * CHUNK, :LANES] for s in range(17)]
    im = [final[s * CHUNK : (s + 1) * CHUNK, LANES:] for s in range(17)]
    first = lax.broadcasted_iota(jnp.int32, (CHUNK, LANES), 1) < LANES // 2
    re[0] = jnp.where(first, re[16], re[0])
    im[0] = jnp.where(first, im[16], im[0])
    return re[:16], im[:16]


def whitened(re, im, small):
    lane = lax.broadcasted_iota(jnp.int32, (CHUNK, LANES), 1)
    first = lane < LANES // 2
    k2 = lane % (LANES // 2)
    size = [jnp.sqrt(a * a + b * b) for a, b in zip(re, im)]
    running = [jnp.zeros_like(size[0])]
    for s in range(1, SLABS):
        running.append(running[-1] + size[s])
    total = running[15] + size[0]
    total = total + pltpu.roll(total, LANES // 2, 1)
    centre = (
        total
        + jnp.where(k2 >= 1, pltpu.roll(total, 1, 1), 0.0)
        + jnp.where(k2 <= 62, pltpu.roll(total, LANES - 1, 1), 0.0)
    )
    before = pltpu.roll(running[15] + size[0], LANES // 2, 1) + running[15]
    out = []
    for s in range(SLABS):
        if s == 0:
            prefix = jnp.where(first, running[15] + size[0], total)
            suffix = jnp.where(first, total - running[15], size[0])
        else:
            prefix = jnp.where(first, running[s], before - running[s - 1])
            suffix = jnp.where(first, total - running[s - 1], running[s] + size[0])
        window = (
            centre
            + jnp.where(k2 >= 2, pltpu.roll(suffix, 2, 1), 0.0)
            + jnp.where(k2 <= 61, pltpu.roll(prefix, LANES - 2, 1), 0.0)
        )
        counted = small[34 + s : 35 + s, :]
        scale = counted / (window + EPSILON * counted)
        out.append((re[s] * scale, im[s] * scale))
    return out


def kernel(
    rows,
    traces,
    pair_list,
    live,
    forward_hbm,
    inverse_hbm,
    small_hbm,
    out_ref,
    x_ref,
    forward,
    inverse,
    small,
    turn,
    ext,
    cross_out,
    cross_own,
    cross_in,
    load_sem,
    table_sem,
    send_sem,
    recv_sem,
    swap_sem,
):
    me = lax.axis_index("pair")
    core = lax.axis_index("tm")
    count = lax.axis_size("pair")
    chunks = rows // CHUNK
    loads = [
        pltpu.make_async_copy(
            traces.at[pl.ds(i * CHUNK * RADIX, CHUNK * RADIX)],
            x_ref.at[pl.ds(i * CHUNK * RADIX, CHUNK * RADIX)],
            load_sem.at[i],
        )
        for i in range(chunks)
    ]
    table_loads = [
        pltpu.make_async_copy(src, dst, table_sem.at[i])
        for i, (src, dst) in enumerate(
            [(small_hbm, small), (forward_hbm, forward), (inverse_hbm, inverse)]
        )
    ]
    loads[0].start()
    table_loads[0].start()
    table_loads[1].start()
    for copy in loads[1:]:
        copy.start()
    table_loads[2].start()

    before, after = lax.rem(me + count - 1, count), lax.rem(me + 1, count)
    barrier = pltpu.get_barrier_semaphore()
    for target in ((before, core), (after, core), (me, 1 - core)):
        pl.semaphore_signal(barrier, inc=1, device_id=target, device_id_type=MESH)

    sends = []
    for i in range(chunks):
        loads[i].wait()
        if i == 0:
            table_loads[0].wait()
            table_loads[1].wait()
        re, im = spectra(x_ref, small, forward, i * CHUNK)
        for s, (a, b) in enumerate(whitened(re, im, small)):
            place = i * CHUNK * 32 + s // 8 * 16 + s % 8
            turn[pl.ds(place, CHUNK, stride=32), :] = a
            turn[pl.ds(place + 8, CHUNK, stride=32), :] = b
        own = pl.ds(rows + i * CHUNK, CHUNK)
        part = turn[pl.ds(i * CHUNK * 32, CHUNK * 32), :].reshape(CHUNK, 2, 16, LANES)
        ext[own] = part.astype(jnp.bfloat16)
        if i == 0:
            pl.semaphore_wait(barrier, 3)
        for way, (target, place) in enumerate(((before, 2 * rows), (after, 0))):
            copy = pltpu.make_async_remote_copy(
                src_ref=ext.at[own],
                dst_ref=ext.at[pl.ds(place + i * CHUNK, CHUNK)],
                send_sem=send_sem.at[way, i],
                recv_sem=recv_sem.at[way, i],
                device_id=(target, core),
                device_id_type=MESH,
            )
            copy.start()
            sends.append(copy)
    for copy in sends:
        copy.wait()

    anchor = me * rows - rows
    kept = rows // 2

    def cross(into, slot, i):
        first = jnp.clip(pair_list[slot, 0] - anchor, 0, 3 * rows - 1)
        second = jnp.clip(pair_list[slot, 1] - anchor, 0, 3 * rows - 1)
        for g in range(2):
            a = ext[first, g].astype(jnp.float32)
            b = ext[second, g].astype(jnp.float32)
            ar, ai, br, bi = a[:8], a[8:], b[:8], b[8:]
            place = pl.ds(g * 8 * kept + i, 8, stride=kept)
            into[0, place, :] = ar * br + ai * bi
            into[1, place, :] = ai * br - ar * bi

    for i in range(kept):
        cross(cross_out, (1 - core) * kept + i, i)
    swap = pltpu.make_async_remote_copy(
        src_ref=cross_out,
        dst_ref=cross_in,
        send_sem=swap_sem.at[0],
        recv_sem=swap_sem.at[1],
        device_id=(me, 1 - core),
        device_id_type=MESH,
    )
    swap.start()
    for i in range(kept):
        cross(cross_own, core * kept + i, i)
    table_loads[2].wait()
    swap.wait()

    both = jnp.concatenate(
        [cross_own[0] + cross_in[0], cross_own[1] + cross_in[1]], axis=1
    )
    lane = lax.broadcasted_iota(jnp.int32, (kept, 2 * LANES), 1) % LANES
    zeroth = both[:kept]
    spread = jnp.concatenate(
        [
            jnp.where(lane < LANES // 2, 0.0, zeroth),
            both[kept:],
            jnp.where(lane < LANES // 2, zeroth, 0.0),
        ],
        axis=0,
    )
    lags = dot3(spread, inverse)
    for part in range(kept // 8):
        bins = []
        for s in range(17):
            place = slice(s * kept + part * 8, s * kept + part * 8 + 8)
            vr, vi = lags[place, :LANES], lags[place, LANES:]
            c, n = small[s : s + 1, :], small[17 + s : 18 + s, :]
            if s == 0:
                bins.append((vr, None))
            elif s == 16:
                bins.append((vr * c - vi * n, None))
            else:
                bins.append((vr * c - vi * n, vr * n + vi * c))
        blocks = real_sum(bins, RADIX, [l1 % RADIX for l1 in range(-8, 8)])
        slot = core * kept + part * 8 + lax.broadcasted_iota(jnp.int32, (8, LANES), 0)
        wanted = slot < live[0]
        for l1 in range(-8, 8):
            out_ref[part * 8 : part * 8 + 8, (l1 + 8) * LANES : (l1 + 9) * LANES] = jnp.where(
                wanted, blocks[l1 % RADIX], 0.0
            )


def shards(traces, pair_list, live_pairs):
    rows = traces.shape[0]
    kept = rows // 2
    chunks = rows // CHUNK
    forward, inverse, small = tables()
    any_space = pl.BlockSpec(memory_space=pl.ANY)
    scalars = pl.BlockSpec(memory_space=pltpu.SMEM)
    f32, bf16 = jnp.float32, jnp.bfloat16
    return pl.pallas_call(
        functools.partial(kernel, rows),
        out_shape=jax.ShapeDtypeStruct((kept, NLAG), f32),
        in_specs=[any_space, scalars, scalars, any_space, any_space, any_space],
        out_specs=pl.BlockSpec(memory_space=pltpu.VMEM),
        scratch_shapes=[
            pltpu.VMEM((rows * RADIX, LANES), f32),
            pltpu.VMEM(forward.shape, bf16),
            pltpu.VMEM(inverse.shape, bf16),
            pltpu.VMEM(small.shape, f32),
            pltpu.VMEM((rows * 32, LANES), f32),
            pltpu.VMEM((3 * rows, 2, 16, LANES), bf16),
            pltpu.VMEM((2, SLABS * kept, LANES), f32),
            pltpu.VMEM((2, SLABS * kept, LANES), f32),
            pltpu.VMEM((2, SLABS * kept, LANES), f32),
            pltpu.SemaphoreType.DMA((chunks,)),
            pltpu.SemaphoreType.DMA((3,)),
            pltpu.SemaphoreType.DMA((2, chunks)),
            pltpu.SemaphoreType.DMA((2, chunks)),
            pltpu.SemaphoreType.DMA((2,)),
        ],
        compiler_params=pltpu.CompilerParams(
            collective_id=0, has_side_effects=True, vmem_limit_bytes=32 * 1024 * 1024
        ),
        name="correlate",
    )(
        traces.reshape(rows * RADIX, LANES),
        pair_list,
        live_pairs,
        jnp.asarray(forward),
        jnp.asarray(inverse),
        jnp.asarray(small),
    )


def solution(mesh):
    placed = (P("pair", "tm", None), P("pair", None), P("pair"))
    return jax.shard_map(
        shards, mesh=mesh, in_specs=placed, out_specs=P(("pair", "tm"), None), check_vma=False
    )
```

time: 94.9 us -> 32.7 us (0.34)
  waiting for transfers between devices: 32 us -> 0 us
  matrix products: 29.4 us -> 0 us
  Pallas kernels: 0 us -> 26.6 us
  between operations: 14.3 us -> 0.67 us
  starting transfers between devices: 5.26 us -> 0 us
  local copies, waits for them, and re-layouts: 9.56 us -> 5.1 us
  other arithmetic: 4.07 us -> 0 us
    dot_general x20 -> x0, matrix products: 29.4 us -> none  [the longest x1 4.42 us: forward_bins(): jnp.einsum('cskm,jm->csjk', turned_imag, sine, precision=HIGHEST)]
    reduce_scatter x1 -> x0, waiting for transfers between devices: 26.9 us -> none  [shards(): return lax.psum_scatter(partial_lags, 'tm', scatter_dimension=0, tiled=True)]
    pallas_call x0 -> x1, Pallas kernels: none -> 26.6 us  [shards(): pl.pallas_call(functools.partial(kernel, rows), out_shape=jax.ShapeDtypeS...]
    reshape x4 -> x0, local copies, waits for them, and re-layouts: 5.88 us -> none  [the longest x1 2.38 us: forward_bins(): final_imag = final_imag.reshape(channels, segments, NT)[..., 1:FB + 1]]
    ppermute x2 -> x0, starting transfers between devices: 5.25 us -> none  [the longest x1 3.96 us: extended_2(): lax.ppermute(tail, axis, [(i, (i + 1) % count) for i in range(ends)])]
    unnamed x4 -> x12, local copies, waits for them, and re-layouts: 0.01 us -> 5.1 us
    ppermute x2 -> x0, waiting for transfers between devices: 5.09 us -> none  [the longest x1 3.83 us: extended_2(): lax.ppermute(head, axis, [((i + 1) % count, i) for i in range(ends)])]
    unnamed x1 -> x0, other arithmetic: 2.3 us -> none
  transfers between devices with their start and end apart: 3 -> 0, of which waited for: 3 -> 0; matrix products, arithmetic and copies ran while one was open for 0% -> 0% of each run, Pallas kernels for 0% -> 0%
where the time goes in v1:
time: 32.7 us; the launch traced here: 32.4 us
  Pallas kernels  26.6 us (81%)
  local copies, waits for them, and re-layouts  5.1 us (16%)
  between operations  0.67 us (2%)
    pallas_call x1, Pallas kernels, shards(): pl.pallas_call(functools.partial(kernel, rows), out_shape=jax.ShapeDtypeS...  26.6 us
    unnamed x12, local copies, waits for them, and re-layouts  5.1 us

profile of v1, /device:TPU:1, one launch (start us, length us, event | category | flops | bytes accessed | tf_op | source)
XLA Modules:
  0.0 32.4 jit_solution(6780039742029216378)
XLA Ops:
  0.7 0.0 copy-start.4
  0.7 0.7 %copy-done.4 = s32[32,2]{0,1:T(2,128)S(1)} copy-done((s32[32,2]{0,1:T(2,128)S(1)}, s32[32,2]{0,1:T(2,128)}, u32[]{:S(2)}) %copy-start.4) | copy-done | bytes 280
  1.3 0.1 copy.7.pair_list
  1.4 0.0 copy-start
  1.4 1.0 %copy-done = f32[32,1,4096]{2,1,0:T(1,128)S(1)} copy-done((f32[32,1,4096]{2,1,0:T(1,128)S(1)}, f32[32,1,4096]{2,1,0:T(1,128)}, u32[]{:S(2)}) %copy-start) | copy-done | bytes 524312
  2.5 0.0 copy-start.1
  2.5 0.9 %copy-done.1 = bf16[2,256,256]{2,1,0:T(8,128)(2,1)S(1)} copy-done((bf16[2,256,256]{2,1,0:T(8,128)(2,1)S(1)}, bf16[2,256,256]{2,1,0:T(8,128)(2,1)}, u32[]{:S(2)}) %copy-start.1) | copy-done | bytes 262168
  3.4 0.0 copy-start.2
  3.4 0.9 %copy-done.2 = bf16[2,256,256]{2,1,0:T(8,128)(2,1)S(1)} copy-done((bf16[2,256,256]{2,1,0:T(8,128)(2,1)S(1)}, bf16[2,256,256]{2,1,0:T(8,128)(2,1)}, u32[]{:S(2)}) %copy-start.2) | copy-done | bytes 262168
  4.4 0.0 copy-start.3
  4.4 0.7 %copy-done.3 = f32[56,128]{1,0:T(8,128)S(1)} copy-done((f32[56,128]{1,0:T(8,128)S(1)}, f32[56,128]{1,0:T(8,128)}, u32[]{:S(2)}) %copy-start.3) | copy-done | bytes 28696
  5.1 26.6 %correlate.1 = f32[16,2048]{1,0:T(8,128)S(1)} custom-call(f32[1024,128]{1,0:T(8,128)S(1)} %bitcast.1, s32[32,2]{1,0:T(8,128)S(1)} %copy.7.pair_list, s32[1]{0:T(128)S(6)} %copy.9.live, bf16[2,256,256]{2,1,0:T(8,128)(2,1)S(1)} %copy-done.2, bf16[2,256,256]{2,1,0:T(8,128)(2,1)S(1)} %copy-done.1, f32[56,128]{1,0:T(8,128)S(1)} %copy-done.3), custom_call_target="tpu_custom_call" | custom-call | tf_op jit(solution)/shard_map/correlate/pallas_call | solution.py:337
  31.8 0.7 %copy.10 = f32[16,2048]{1,0:T(8,128)} copy(f32[16,2048]{1,0:T(8,128)S(1)} %correlate.1) | data formatting | bytes 262144
Async XLA Ops:
  0.7 0.7 %copy-start.4 = (s32[32,2]{0,1:T(2,128)S(1)}, s32[32,2]{0,1:T(2,128)}, u32[]{:S(2)}) copy-start(s32[32,2]{0,1:T(2,128)} %param.7) | copy-start | bytes 772
  1.4 1.0 %copy-start = (f32[32,1,4096]{2,1,0:T(1,128)S(1)}, f32[32,1,4096]{2,1,0:T(1,128)}, u32[]{:S(2)}) copy-start(f32[32,1,4096]{2,1,0:T(1,128)} %param.6) | copy-start | bytes 1572868
  2.5 0.9 %copy-start.1 = (bf16[2,256,256]{2,1,0:T(8,128)(2,1)S(1)}, bf16[2,256,256]{2,1,0:T(8,128)(2,1)}, u32[]{:S(2)}) copy-start(bf16[2,256,256]{2,1,0:T(8,128)(2,1)} %constant.7.clone.inverse_hbm) | copy-start | bytes 786436
  3.4 0.9 %copy-start.2 = (bf16[2,256,256]{2,1,0:T(8,128)(2,1)S(1)}, bf16[2,256,256]{2,1,0:T(8,128)(2,1)}, u32[]{:S(2)}) copy-start(bf16[2,256,256]{2,1,0:T(8,128)(2,1)} %constant.6.clone.forward_hbm) | copy-start | bytes 786436
  4.4 0.7 %copy-start.3 = (f32[56,128]{1,0:T(8,128)S(1)}, f32[56,128]{1,0:T(8,128)}, u32[]{:S(2)}) copy-start(f32[56,128]{1,0:T(8,128)} %constant.8.clone.small_hbm) | copy-start | bytes 86020

commit v2 on v1

--- a/solution.py
+++ b/solution.py
@@ -181,11 +181,13 @@
     rows,
     traces,
     pair_list,
-    live,
+    live_pairs,
     forward_hbm,
     inverse_hbm,
     small_hbm,
     out_ref,
+    members,
+    live,
     x_ref,
     forward,
     inverse,
@@ -216,7 +218,13 @@
     table_loads = [
         pltpu.make_async_copy(src, dst, table_sem.at[i])
         for i, (src, dst) in enumerate(
-            [(small_hbm, small), (forward_hbm, forward), (inverse_hbm, inverse)]
+            [
+                (small_hbm, small),
+                (forward_hbm, forward),
+                (inverse_hbm, inverse),
+                (pair_list, members),
+                (live_pairs, live),
+            ]
         )
     ]
     loads[0].start()
@@ -224,14 +232,30 @@
     table_loads[1].start()
     for copy in loads[1:]:
         copy.start()
-    table_loads[2].start()
-
-    before, after = lax.rem(me + count - 1, count), lax.rem(me + 1, count)
+    for copy in table_loads[2:]:
+        copy.start()
+
     barrier = pltpu.get_barrier_semaphore()
-    for target in ((before, core), (after, core), (me, 1 - core)):
+
+    def greet(target):
         pl.semaphore_signal(barrier, inc=1, device_id=target, device_id_type=MESH)
 
-    sends = []
+    has_before, has_after = me > 0, me < count - 1
+    pl.when(has_before)(lambda: greet((me - 1, core)))
+    pl.when(has_after)(lambda: greet((me + 1, core)))
+    greet((me, 1 - core))
+
+    def send(way, i):
+        step, place = ((-1, 2 * rows), (1, 0))[way]
+        return pltpu.make_async_remote_copy(
+            src_ref=ext.at[pl.ds(rows + i * CHUNK, CHUNK)],
+            dst_ref=ext.at[pl.ds(place + i * CHUNK, CHUNK)],
+            send_sem=send_sem.at[way, i],
+            recv_sem=recv_sem.at[way, i],
+            device_id=(me + step, core),
+            device_id_type=MESH,
+        )
+
     for i in range(chunks):
         loads[i].wait()
         if i == 0:
@@ -246,27 +270,28 @@
         part = turn[pl.ds(i * CHUNK * 32, CHUNK * 32), :].reshape(CHUNK, 2, 16, LANES)
         ext[own] = part.astype(jnp.bfloat16)
         if i == 0:
-            pl.semaphore_wait(barrier, 3)
-        for way, (target, place) in enumerate(((before, 2 * rows), (after, 0))):
-            copy = pltpu.make_async_remote_copy(
-                src_ref=ext.at[own],
-                dst_ref=ext.at[pl.ds(place + i * CHUNK, CHUNK)],
-                send_sem=send_sem.at[way, i],
-                recv_sem=recv_sem.at[way, i],
-                device_id=(target, core),
-                device_id_type=MESH,
-            )
-            copy.start()
-            sends.append(copy)
-    for copy in sends:
-        copy.wait()
-
+            pl.semaphore_wait(barrier, 1 + has_before.astype(jnp.int32) + has_after.astype(jnp.int32))
+        pl.when(has_before)(lambda: send(0, i).start())
+        pl.when(has_after)(lambda: send(1, i).start())
+
+    @pl.when(has_after)
+    def _():
+        for i in range(chunks):
+            send(0, i).wait_recv()
+
+    @pl.when(has_before)
+    def _():
+        for i in range(chunks):
+            send(1, i).wait_recv()
+
+    table_loads[3].wait()
+    table_loads[4].wait()
     anchor = me * rows - rows
     kept = rows // 2
 
     def cross(into, slot, i):
-        first = jnp.clip(pair_list[slot, 0] - anchor, 0, 3 * rows - 1)
-        second = jnp.clip(pair_list[slot, 1] - anchor, 0, 3 * rows - 1)
+        first = jnp.clip(members[0, slot] - anchor, 0, 3 * rows - 1)
+        second = jnp.clip(members[1, slot] - anchor, 0, 3 * rows - 1)
         for g in range(2):
             a = ext[first, g].astype(jnp.float32)
             b = ext[second, g].astype(jnp.float32)
@@ -325,21 +350,32 @@
                 wanted, blocks[l1 % RADIX], 0.0
             )
 
+    @pl.when(has_before)
+    def _():
+        for i in range(chunks):
+            send(0, i).wait_send()
+
+    @pl.when(has_after)
+    def _():
+        for i in range(chunks):
+            send(1, i).wait_send()
+
 
 def shards(traces, pair_list, live_pairs):
     rows = traces.shape[0]
     kept = rows // 2
     chunks = rows // CHUNK
     forward, inverse, small = tables()
-    any_space = pl.BlockSpec(memory_space=pl.ANY)
-    scalars = pl.BlockSpec(memory_space=pltpu.SMEM)
+    in_hbm = pl.BlockSpec(memory_space=pltpu.HBM)
     f32, bf16 = jnp.float32, jnp.bfloat16
     return pl.pallas_call(
         functools.partial(kernel, rows),
         out_shape=jax.ShapeDtypeStruct((kept, NLAG), f32),
-        in_specs=[any_space, scalars, scalars, any_space, any_space, any_space],
+        in_specs=[in_hbm] * 6,
         out_specs=pl.BlockSpec(memory_space=pltpu.VMEM),
         scratch_shapes=[
+            pltpu.SMEM((2, rows), jnp.int32),
+            pltpu.SMEM((1,), jnp.int32),
             pltpu.VMEM((rows * RADIX, LANES), f32),
             pltpu.VMEM(forward.shape, bf16),
             pltpu.VMEM(inverse.shape, bf16),
@@ -350,18 +386,18 @@
             pltpu.VMEM((2, SLABS * kept, LANES), f32),
             pltpu.VMEM((2, SLABS * kept, LANES), f32),
             pltpu.SemaphoreType.DMA((chunks,)),
-            pltpu.SemaphoreType.DMA((3,)),
+            pltpu.SemaphoreType.DMA((5,)),
             pltpu.SemaphoreType.DMA((2, chunks)),
             pltpu.SemaphoreType.DMA((2, chunks)),
             pltpu.SemaphoreType.DMA((2,)),
         ],
         compiler_params=pltpu.CompilerParams(
-            collective_id=0, has_side_effects=True, vmem_limit_bytes=32 * 1024 * 1024
+            collective_id=0, has_side_effects=True, vmem_limit_bytes=60 * 1024 * 1024
         ),
         name="correlate",
     )(
         traces.reshape(rows * RADIX, LANES),
-        pair_list,
+        pair_list.T,
         live_pairs,
         jnp.asarray(forward),
         jnp.asarray(inverse),

time: 32.7 us -> 19.8 us (0.61)
  the two profiles are of different devices: /device:TPU:1 before, /device:TPU:449 now
where the time goes in v2:
time: 19.8 us; the launch traced here: 19.6 us
  Pallas kernels  17.4 us (88%)
  local copies, waits for them, and re-layouts  1.57 us (8%)
  between operations  0.66 us (3%)
    pallas_call x1, Pallas kernels, shards(): pl.pallas_call(functools.partial(kernel, rows), out_shape=jax.ShapeDtypeS...  17.4 us
    unnamed x1, local copies, waits for them, and re-layouts  1.57 us

profile of v2, /device:TPU:449, one launch (start us, length us, event | category | flops | bytes accessed | tf_op | source)
XLA Modules:
  0.0 19.6 jit_solution(15773760772937106118)
XLA Ops:
  0.7 17.4 %correlate.1 = f32[16,2048]{1,0:T(8,128)} custom-call(f32[1024,128]{1,0:T(8,128)} %bitcast.2, s32[2,32]{1,0:T(2,128)} %bitcast.3, s32[1]{0:T(128)S(6)} %copy.8.live_pairs, bf16[2,256,256]{2,1,0:T(8,128)(2,1)} %constant.6.clone.forward_hbm, bf16[2,256,256]{2,1,0:T(8,128)(2,1)} %constant.7.clone.inverse_hbm, f32[56,128]{1,0:T(8,128)} %constant.8.clone.small_hbm), custom_call_target="tpu_custom_call" | custom-call | tf_op jit(solution)/shard_map/correlate/pallas_call | solution.py:371
  18.0 1.6 %copy.9 = f32[16,2048]{1,0:T(8,128)} copy(f32[16,2048]{1,0:T(8,128)} %correlate.1) | data formatting | bytes 262144

commit v3 on v2

--- a/solution.py
+++ b/solution.py
@@ -117,7 +117,8 @@
 
 
 def spectra(x_ref, small, forward, base):
-    values = [x_ref[pl.ds(base * RADIX + n1, CHUNK, stride=RADIX), :] for n1 in range(RADIX)]
+    first = pl.multiple_of(base * RADIX, CHUNK * RADIX)
+    values = [x_ref[pl.ds(first + n1, CHUNK, stride=RADIX), :] for n1 in range(RADIX)]
     turned_re, turned_im = [], []
     for s, (re, im) in enumerate(real_dft(values)):
         c, n = small[s : s + 1, :], small[17 + s : 18 + s, :]
@@ -193,7 +194,8 @@
     inverse,
     small,
     turn,
-    ext,
+    ext_0,
+    ext_1,
     cross_out,
     cross_own,
     cross_in,
@@ -207,14 +209,14 @@
     core = lax.axis_index("tm")
     count = lax.axis_size("pair")
     chunks = rows // CHUNK
-    loads = [
-        pltpu.make_async_copy(
-            traces.at[pl.ds(i * CHUNK * RADIX, CHUNK * RADIX)],
-            x_ref.at[pl.ds(i * CHUNK * RADIX, CHUNK * RADIX)],
-            load_sem.at[i],
-        )
-        for i in range(chunks)
-    ]
+    kept = rows // 2
+    ext = (ext_0, ext_1)
+
+    def load(i):
+        size = CHUNK * RADIX
+        place = pl.ds(pl.multiple_of(i * size, size), size)
+        return pltpu.make_async_copy(traces.at[place], x_ref.at[place], load_sem.at[i])
+
     table_loads = [
         pltpu.make_async_copy(src, dst, table_sem.at[i])
         for i, (src, dst) in enumerate(
@@ -227,109 +229,125 @@
             ]
         )
     ]
-    loads[0].start()
+    load(0).start()
     table_loads[0].start()
     table_loads[1].start()
-    for copy in loads[1:]:
-        copy.start()
+    for i in range(1, chunks):
+        load(i).start()
     for copy in table_loads[2:]:
         copy.start()
 
+    first = (me == 0).astype(jnp.int32)
+    last = (me == count - 1).astype(jnp.int32)
+    other = 1 - core
+    ways = (
+        ((me - 1 + first, core + first * (other - core)), 2 * rows * (1 - first), first),
+        ((me + 1 - last, core + last * (other - core)), 2 * rows * last, 1 - last),
+    )
     barrier = pltpu.get_barrier_semaphore()
-
-    def greet(target):
+    for target in (ways[0][0], ways[1][0], (me, other)):
         pl.semaphore_signal(barrier, inc=1, device_id=target, device_id_type=MESH)
 
-    has_before, has_after = me > 0, me < count - 1
-    pl.when(has_before)(lambda: greet((me - 1, core)))
-    pl.when(has_after)(lambda: greet((me + 1, core)))
-    greet((me, 1 - core))
-
-    def send(way, i):
-        step, place = ((-1, 2 * rows), (1, 0))[way]
+    def send(way, part):
+        target, place, semaphore = ways[way]
+        whole = isinstance(part, int) and part == chunks
+        half, start, size = (1, 0, rows) if whole else (0, part * CHUNK, CHUNK)
         return pltpu.make_async_remote_copy(
-            src_ref=ext.at[pl.ds(rows + i * CHUNK, CHUNK)],
-            dst_ref=ext.at[pl.ds(place + i * CHUNK, CHUNK)],
-            send_sem=send_sem.at[way, i],
-            recv_sem=recv_sem.at[way, i],
-            device_id=(me + step, core),
+            src_ref=ext[half].at[pl.ds(rows + start, size)],
+            dst_ref=ext[half].at[pl.ds(place + start, size)],
+            send_sem=send_sem.at[way, part],
+            recv_sem=recv_sem.at[semaphore, part],
+            device_id=target,
             device_id_type=MESH,
         )
 
-    for i in range(chunks):
-        loads[i].wait()
-        if i == 0:
-            table_loads[0].wait()
-            table_loads[1].wait()
-        re, im = spectra(x_ref, small, forward, i * CHUNK)
+    def arrival(side, part):
+        half, start, size = (0, part * CHUNK, CHUNK) if part < chunks else (1, 0, rows)
+        place = ext[half].at[pl.ds((1 - side) * 2 * rows + start, size)]
+        return pltpu.make_async_remote_copy(
+            src_ref=place,
+            dst_ref=place,
+            send_sem=send_sem.at[0, part],
+            recv_sem=recv_sem.at[side, part],
+            device_id=(me, other),
+            device_id_type=MESH,
+        )
+
+    table_loads[0].wait()
+    table_loads[1].wait()
+
+    def transform(i, carry):
+        start = pl.multiple_of(i * CHUNK, CHUNK)
+        load(i).wait()
+        re, im = spectra(x_ref, small, forward, start)
         for s, (a, b) in enumerate(whitened(re, im, small)):
-            place = i * CHUNK * 32 + s // 8 * 16 + s % 8
+            place = s // 8 * 16 + s % 8
             turn[pl.ds(place, CHUNK, stride=32), :] = a
             turn[pl.ds(place + 8, CHUNK, stride=32), :] = b
-        own = pl.ds(rows + i * CHUNK, CHUNK)
-        part = turn[pl.ds(i * CHUNK * 32, CHUNK * 32), :].reshape(CHUNK, 2, 16, LANES)
-        ext[own] = part.astype(jnp.bfloat16)
-        if i == 0:
-            pl.semaphore_wait(barrier, 1 + has_before.astype(jnp.int32) + has_after.astype(jnp.int32))
-        pl.when(has_before)(lambda: send(0, i).start())
-        pl.when(has_after)(lambda: send(1, i).start())
-
-    @pl.when(has_after)
-    def _():
-        for i in range(chunks):
-            send(0, i).wait_recv()
-
-    @pl.when(has_before)
-    def _():
-        for i in range(chunks):
-            send(1, i).wait_recv()
+        part = turn[...].reshape(CHUNK, 2, 16, LANES)
+        for half in range(2):
+            ext[half][pl.ds(rows + start, CHUNK)] = part[:, half].astype(jnp.bfloat16)
+
+        @pl.when(i == 0)
+        def _():
+            pl.semaphore_wait(barrier, 3)
+
+        for way in range(2):
+            send(way, i).start()
+        return carry
+
+    lax.fori_loop(0, chunks, transform, 0)
+    for way in range(2):
+        send(way, chunks).start()
 
     table_loads[3].wait()
     table_loads[4].wait()
     anchor = me * rows - rows
-    kept = rows // 2
-
-    def cross(into, slot, i):
-        first = jnp.clip(members[0, slot] - anchor, 0, 3 * rows - 1)
-        second = jnp.clip(members[1, slot] - anchor, 0, 3 * rows - 1)
-        for g in range(2):
-            a = ext[first, g].astype(jnp.float32)
-            b = ext[second, g].astype(jnp.float32)
-            ar, ai, br, bi = a[:8], a[8:], b[:8], b[8:]
-            place = pl.ds(g * 8 * kept + i, 8, stride=kept)
-            into[0, place, :] = ar * br + ai * bi
-            into[1, place, :] = ai * br - ar * bi
-
-    for i in range(kept):
-        cross(cross_out, (1 - core) * kept + i, i)
-    swap = pltpu.make_async_remote_copy(
-        src_ref=cross_out,
-        dst_ref=cross_in,
-        send_sem=swap_sem.at[0],
-        recv_sem=swap_sem.at[1],
-        device_id=(me, 1 - core),
-        device_id_type=MESH,
-    )
-    swap.start()
-    for i in range(kept):
-        cross(cross_own, core * kept + i, i)
+
+    def cross(half, into, slot, i):
+        one = jnp.clip(members[0, slot] - anchor, 0, 3 * rows - 1)
+        two = jnp.clip(members[1, slot] - anchor, 0, 3 * rows - 1)
+        a = ext[half][one].astype(jnp.float32)
+        b = ext[half][two].astype(jnp.float32)
+        ar, ai, br, bi = a[:8], a[8:], b[:8], b[8:]
+        place = pl.ds(i, 8, stride=kept)
+        into[half, 0, place, :] = ar * br + ai * bi
+        into[half, 1, place, :] = ai * br - ar * bi
+
+    def swap(half):
+        return pltpu.make_async_remote_copy(
+            src_ref=cross_out.at[half],
+            dst_ref=cross_in.at[half],
+            send_sem=swap_sem.at[0, half],
+            recv_sem=swap_sem.at[1, half],
+            device_id=(me, other),
+            device_id_type=MESH,
+        )
+
+    for half in range(2):
+        for side in range(2):
+            for part in range(chunks) if half == 0 else [chunks]:
+                arrival(side, part).wait_recv()
+        for i in range(kept):
+            cross(half, cross_out, other * kept + i, i)
+        swap(half).start()
+        for i in range(kept):
+            cross(half, cross_own, core * kept + i, i)
     table_loads[2].wait()
-    swap.wait()
-
-    both = jnp.concatenate(
-        [cross_own[0] + cross_in[0], cross_own[1] + cross_in[1]], axis=1
-    )
+
     lane = lax.broadcasted_iota(jnp.int32, (kept, 2 * LANES), 1) % LANES
-    zeroth = both[:kept]
-    spread = jnp.concatenate(
-        [
-            jnp.where(lane < LANES // 2, 0.0, zeroth),
-            both[kept:],
-            jnp.where(lane < LANES // 2, zeroth, 0.0),
-        ],
-        axis=0,
-    )
-    lags = dot3(spread, inverse)
+    parts = []
+    for half in range(2):
+        swap(half).wait()
+        both = jnp.concatenate(
+            [cross_own[half, i] + cross_in[half, i] for i in range(2)], axis=1
+        )
+        if half == 0:
+            zeroth = both[:kept]
+            parts += [jnp.where(lane < LANES // 2, 0.0, zeroth), both[kept:]]
+        else:
+            parts += [both, jnp.where(lane < LANES // 2, zeroth, 0.0)]
+    lags = dot3(jnp.concatenate(parts, axis=0), inverse)
     for part in range(kept // 8):
         bins = []
         for s in range(17):
@@ -349,16 +367,9 @@
             out_ref[part * 8 : part * 8 + 8, (l1 + 8) * LANES : (l1 + 9) * LANES] = jnp.where(
                 wanted, blocks[l1 % RADIX], 0.0
             )
-
-    @pl.when(has_before)
-    def _():
-        for i in range(chunks):
-            send(0, i).wait_send()
-
-    @pl.when(has_after)
-    def _():
-        for i in range(chunks):
-            send(1, i).wait_send()
+    for way in range(2):
+        for part in range(chunks + 1):
+            send(way, part).wait_send()
 
 
 def shards(traces, pair_list, live_pairs):
@@ -366,6 +377,7 @@
     kept = rows // 2
     chunks = rows // CHUNK
     forward, inverse, small = tables()
+    in_place = functools.partial(pltpu.with_memory_space_constraint, memory_space=pltpu.HBM)
     in_hbm = pl.BlockSpec(memory_space=pltpu.HBM)
     f32, bf16 = jnp.float32, jnp.bfloat16
     return pl.pallas_call(
@@ -380,28 +392,29 @@
             pltpu.VMEM(forward.shape, bf16),
             pltpu.VMEM(inverse.shape, bf16),
             pltpu.VMEM(small.shape, f32),
-            pltpu.VMEM((rows * 32, LANES), f32),
-            pltpu.VMEM((3 * rows, 2, 16, LANES), bf16),
-            pltpu.VMEM((2, SLABS * kept, LANES), f32),
-            pltpu.VMEM((2, SLABS * kept, LANES), f32),
-            pltpu.VMEM((2, SLABS * kept, LANES), f32),
+            pltpu.VMEM((CHUNK * 32, LANES), f32),
+            pltpu.VMEM((3 * rows, 16, LANES), bf16),
+            pltpu.VMEM((3 * rows, 16, LANES), bf16),
+            pltpu.VMEM((2, 2, 8 * kept, LANES), f32),
+            pltpu.VMEM((2, 2, 8 * kept, LANES), f32),
+            pltpu.VMEM((2, 2, 8 * kept, LANES), f32),
             pltpu.SemaphoreType.DMA((chunks,)),
             pltpu.SemaphoreType.DMA((5,)),
-            pltpu.SemaphoreType.DMA((2, chunks)),
-            pltpu.SemaphoreType.DMA((2, chunks)),
-            pltpu.SemaphoreType.DMA((2,)),
+            pltpu.SemaphoreType.DMA((2, chunks + 1)),
+            pltpu.SemaphoreType.DMA((2, chunks + 1)),
+            pltpu.SemaphoreType.DMA((2, 2)),
         ],
         compiler_params=pltpu.CompilerParams(
-            collective_id=0, has_side_effects=True, vmem_limit_bytes=60 * 1024 * 1024
+            collective_id=0, has_side_effects=True, vmem_limit_bytes=32 * 1024 * 1024
         ),
         name="correlate",
     )(
-        traces.reshape(rows * RADIX, LANES),
-        pair_list.T,
+        in_place(traces.reshape(rows * RADIX, LANES)),
+        in_place(pair_list.T),
         live_pairs,
-        jnp.asarray(forward),
-        jnp.asarray(inverse),
-        jnp.asarray(small),
+        in_place(jnp.asarray(forward)),
+        in_place(jnp.asarray(inverse)),
+        in_place(jnp.asarray(small)),
     )
 
 

time: 19.8 us -> 18.3 us (0.924)
  local copies, waits for them, and re-layouts: 1.57 us -> 0.66 us
  Pallas kernels: 17.4 us -> 16.8 us
    unnamed x1, local copies, waits for them, and re-layouts: 1.57 us -> 0.66 us
    pallas_call x1, Pallas kernels: 17.4 us -> 16.8 us  [shards(): pl.pallas_call(functools.partial(kernel, rows), out_shape=jax.ShapeDtypeS...]
where the time goes in v3:
time: 18.3 us; the launch traced here: 18.1 us
  Pallas kernels  16.8 us (92%)
  local copies, waits for them, and re-layouts  0.66 us (4%)
  between operations  0.66 us (4%)
    pallas_call x1, Pallas kernels, shards(): pl.pallas_call(functools.partial(kernel, rows), out_shape=jax.ShapeDtypeS...  16.8 us
    unnamed x1, local copies, waits for them, and re-layouts  0.66 us

profile of v3, /device:TPU:449, one launch (start us, length us, event | category | flops | bytes accessed | tf_op | source)
XLA Modules:
  0.0 18.1 jit_solution(3999415250890835218)
XLA Ops:
  0.7 16.8 %correlate.1 = f32[16,2048]{1,0:T(8,128)S(1)} custom-call(f32[1024,128]{1,0:T(8,128)} %bitcast.2, s32[2,32]{1,0:T(2,128)} %bitcast.3, s32[1]{0:T(128)S(6)} %copy.8.live_pairs, bf16[2,256,256]{2,1,0:T(8,128)(2,1)} %constant.6.clone.forward_hbm, bf16[2,256,256]{2,1,0:T(8,128)(2,1)} %constant.7.clone.inverse_hbm, f32[56,128]{1,0:T(8,128)} %constant.8.clone.small_hbm), custom_call_target="tpu_custom_call" | custom-call | tf_op jit(solution)/shard_map/correlate/pallas_call | solution.py:383
  17.4 0.7 %copy.9 = f32[16,2048]{1,0:T(8,128)} copy(f32[16,2048]{1,0:T(8,128)S(1)} %correlate.1) | data formatting | bytes 262144

commit v4 on v3

--- a/solution.py
+++ b/solution.py
@@ -213,8 +213,7 @@
     ext = (ext_0, ext_1)
 
     def load(i):
-        size = CHUNK * RADIX
-        place = pl.ds(pl.multiple_of(i * size, size), size)
+        place = (pl.ds(0, CHUNK * RADIX), pl.ds(CHUNK * RADIX, (rows - CHUNK) * RADIX))[i]
         return pltpu.make_async_copy(traces.at[place], x_ref.at[place], load_sem.at[i])
 
     table_loads = [
@@ -232,8 +231,7 @@
     load(0).start()
     table_loads[0].start()
     table_loads[1].start()
-    for i in range(1, chunks):
-        load(i).start()
+    load(1).start()
     for copy in table_loads[2:]:
         copy.start()
 
@@ -248,37 +246,35 @@
     for target in (ways[0][0], ways[1][0], (me, other)):
         pl.semaphore_signal(barrier, inc=1, device_id=target, device_id_type=MESH)
 
-    def send(way, part):
-        target, place, semaphore = ways[way]
-        whole = isinstance(part, int) and part == chunks
-        half, start, size = (1, 0, rows) if whole else (0, part * CHUNK, CHUNK)
+    def send(way, half, start, size):
+        target, place, side = ways[way]
         return pltpu.make_async_remote_copy(
             src_ref=ext[half].at[pl.ds(rows + start, size)],
             dst_ref=ext[half].at[pl.ds(place + start, size)],
-            send_sem=send_sem.at[way, part],
-            recv_sem=recv_sem.at[semaphore, part],
+            send_sem=send_sem.at[way, half],
+            recv_sem=recv_sem.at[side, half],
             device_id=target,
             device_id_type=MESH,
         )
 
-    def arrival(side, part):
-        half, start, size = (0, part * CHUNK, CHUNK) if part < chunks else (1, 0, rows)
-        place = ext[half].at[pl.ds((1 - side) * 2 * rows + start, size)]
+    def arrival(side, half):
+        place = ext[half].at[pl.ds((1 - side) * 2 * rows, rows)]
         return pltpu.make_async_remote_copy(
             src_ref=place,
             dst_ref=place,
-            send_sem=send_sem.at[0, part],
-            recv_sem=recv_sem.at[side, part],
+            send_sem=send_sem.at[0, half],
+            recv_sem=recv_sem.at[side, half],
             device_id=(me, other),
             device_id_type=MESH,
         )
 
+    load(0).wait()
     table_loads[0].wait()
     table_loads[1].wait()
 
     def transform(i, carry):
         start = pl.multiple_of(i * CHUNK, CHUNK)
-        load(i).wait()
+        pl.when(i == 1)(load(1).wait)
         re, im = spectra(x_ref, small, forward, start)
         for s, (a, b) in enumerate(whitened(re, im, small)):
             place = s // 8 * 16 + s % 8
@@ -293,12 +289,18 @@
             pl.semaphore_wait(barrier, 3)
 
         for way in range(2):
-            send(way, i).start()
+            send(way, 0, start, CHUNK).start()
+
+        @pl.when(i > 0)
+        def _():
+            for way in range(2):
+                send(way, 1, start - CHUNK, CHUNK).start()
+
         return carry
 
     lax.fori_loop(0, chunks, transform, 0)
     for way in range(2):
-        send(way, chunks).start()
+        send(way, 1, rows - CHUNK, CHUNK).start()
 
     table_loads[3].wait()
     table_loads[4].wait()
@@ -326,8 +328,7 @@
 
     for half in range(2):
         for side in range(2):
-            for part in range(chunks) if half == 0 else [chunks]:
-                arrival(side, part).wait_recv()
+            arrival(side, half).wait_recv()
         for i in range(kept):
             cross(half, cross_out, other * kept + i, i)
         swap(half).start()
@@ -336,7 +337,7 @@
     table_loads[2].wait()
 
     lane = lax.broadcasted_iota(jnp.int32, (kept, 2 * LANES), 1) % LANES
-    parts = []
+    lags = []
     for half in range(2):
         swap(half).wait()
         both = jnp.concatenate(
@@ -344,10 +345,14 @@
         )
         if half == 0:
             zeroth = both[:kept]
-            parts += [jnp.where(lane < LANES // 2, 0.0, zeroth), both[kept:]]
-        else:
-            parts += [both, jnp.where(lane < LANES // 2, zeroth, 0.0)]
-    lags = dot3(jnp.concatenate(parts, axis=0), inverse)
+            parts = [
+                jnp.where(lane < LANES // 2, 0.0, zeroth),
+                both[kept:],
+                jnp.where(lane < LANES // 2, zeroth, 0.0),
+            ]
+            both = jnp.concatenate(parts, axis=0)
+        lags.append(dot3(both, inverse))
+    lags = jnp.concatenate([lags[0][: 8 * kept], lags[1], lags[0][8 * kept :]], axis=0)
     for part in range(kept // 8):
         bins = []
         for s in range(17):
@@ -368,8 +373,8 @@
                 wanted, blocks[l1 % RADIX], 0.0
             )
     for way in range(2):
-        for part in range(chunks + 1):
-            send(way, part).wait_send()
+        for half in range(2):
+            send(way, half, 0, rows).wait_send()
 
 
 def shards(traces, pair_list, live_pairs):
@@ -398,10 +403,10 @@
             pltpu.VMEM((2, 2, 8 * kept, LANES), f32),
             pltpu.VMEM((2, 2, 8 * kept, LANES), f32),
             pltpu.VMEM((2, 2, 8 * kept, LANES), f32),
-            pltpu.SemaphoreType.DMA((chunks,)),
+            pltpu.SemaphoreType.DMA((2,)),
             pltpu.SemaphoreType.DMA((5,)),
-            pltpu.SemaphoreType.DMA((2, chunks + 1)),
-            pltpu.SemaphoreType.DMA((2, chunks + 1)),
+            pltpu.SemaphoreType.DMA((2, 2)),
+            pltpu.SemaphoreType.DMA((2, 2)),
             pltpu.SemaphoreType.DMA((2, 2)),
         ],
         compiler_params=pltpu.CompilerParams(

time: 18.3 us -> 18.1 us (0.989)
  Pallas kernels: 16.8 us -> 16.6 us
where the time goes in v4:
time: 18.1 us; the launch traced here: 18 us
  Pallas kernels  16.6 us (92%)
  local copies, waits for them, and re-layouts  0.66 us (4%)
  between operations  0.66 us (4%)
    pallas_call x1, Pallas kernels, shards(): pl.pallas_call(functools.partial(kernel, rows), out_shape=jax.ShapeDtypeS...  16.6 us
    unnamed x1, local copies, waits for them, and re-layouts  0.66 us

profile of v4, /device:TPU:449, one launch (start us, length us, event | category | flops | bytes accessed | tf_op | source)
XLA Modules:
  0.0 18.0 jit_solution(6502030804997050710)
XLA Ops:
  0.7 16.6 %correlate.1 = f32[16,2048]{1,0:T(8,128)S(1)} custom-call(f32[1024,128]{1,0:T(8,128)} %bitcast.2, s32[2,32]{1,0:T(2,128)} %bitcast.3, s32[1]{0:T(128)S(6)} %copy.8.live_pairs, bf16[2,256,256]{2,1,0:T(8,128)(2,1)} %constant.6.clone.forward_hbm, bf16[2,256,256]{2,1,0:T(8,128)(2,1)} %constant.7.clone.inverse_hbm, f32[56,128]{1,0:T(8,128)} %constant.8.clone.small_hbm), custom_call_target="tpu_custom_call" | custom-call | tf_op jit(solution)/shard_map/correlate/pallas_call | solution.py:388
  17.3 0.7 %copy.9 = f32[16,2048]{1,0:T(8,128)} copy(f32[16,2048]{1,0:T(8,128)S(1)} %correlate.1) | data formatting | bytes 262144

commit v5 on v4

--- a/solution.py
+++ b/solution.py
@@ -19,6 +19,7 @@
 LANES = 128
 SLABS = 16
 CHUNK = 8
+PITCH = 40
 MESH = pl.DeviceIdType.MESH
 
 
@@ -228,13 +229,6 @@
             ]
         )
     ]
-    load(0).start()
-    table_loads[0].start()
-    table_loads[1].start()
-    load(1).start()
-    for copy in table_loads[2:]:
-        copy.start()
-
     first = (me == 0).astype(jnp.int32)
     last = (me == count - 1).astype(jnp.int32)
     other = 1 - core
@@ -246,6 +240,13 @@
     for target in (ways[0][0], ways[1][0], (me, other)):
         pl.semaphore_signal(barrier, inc=1, device_id=target, device_id_type=MESH)
 
+    load(0).start()
+    table_loads[0].start()
+    table_loads[1].start()
+    load(1).start()
+    for copy in table_loads[2:]:
+        copy.start()
+
     def send(way, half, start, size):
         target, place, side = ways[way]
         return pltpu.make_async_remote_copy(
@@ -278,29 +279,23 @@
         re, im = spectra(x_ref, small, forward, start)
         for s, (a, b) in enumerate(whitened(re, im, small)):
             place = s // 8 * 16 + s % 8
-            turn[pl.ds(place, CHUNK, stride=32), :] = a
-            turn[pl.ds(place + 8, CHUNK, stride=32), :] = b
-        part = turn[...].reshape(CHUNK, 2, 16, LANES)
+            turn[pl.ds(place, CHUNK, stride=PITCH), :] = a
+            turn[pl.ds(place + 8, CHUNK, stride=PITCH), :] = b
+        part = turn[...].reshape(CHUNK, PITCH, LANES)
         for half in range(2):
-            ext[half][pl.ds(rows + start, CHUNK)] = part[:, half].astype(jnp.bfloat16)
+            block = part[:, half * 16 : half * 16 + 16]
+            ext[half][pl.ds(rows + start, CHUNK)] = block.astype(jnp.bfloat16)
 
         @pl.when(i == 0)
         def _():
             pl.semaphore_wait(barrier, 3)
 
-        for way in range(2):
-            send(way, 0, start, CHUNK).start()
-
-        @pl.when(i > 0)
-        def _():
+        for half in range(2):
             for way in range(2):
-                send(way, 1, start - CHUNK, CHUNK).start()
-
+                send(way, half, start, CHUNK).start()
         return carry
 
     lax.fori_loop(0, chunks, transform, 0)
-    for way in range(2):
-        send(way, 1, rows - CHUNK, CHUNK).start()
 
     table_loads[3].wait()
     table_loads[4].wait()
@@ -397,7 +392,7 @@
             pltpu.VMEM(forward.shape, bf16),
             pltpu.VMEM(inverse.shape, bf16),
             pltpu.VMEM(small.shape, f32),
-            pltpu.VMEM((CHUNK * 32, LANES), f32),
+            pltpu.VMEM((CHUNK * PITCH, LANES), f32),
             pltpu.VMEM((3 * rows, 16, LANES), bf16),
             pltpu.VMEM((3 * rows, 16, LANES), bf16),
             pltpu.VMEM((2, 2, 8 * kept, LANES), f32),

time: 18.1 us -> 17.8 us (0.983)
  Pallas kernels: 16.6 us -> 16.4 us
    pallas_call x1, Pallas kernels: 16.6 us -> 16.4 us  [shards(): pl.pallas_call(functools.partial(kernel, rows), out_shape=jax.ShapeDtypeS...]
where the time goes in v5:
time: 17.8 us; the launch traced here: 17.7 us
  Pallas kernels  16.4 us (92%)
  local copies, waits for them, and re-layouts  0.66 us (4%)
  between operations  0.66 us (4%)
    pallas_call x1, Pallas kernels, shards(): pl.pallas_call(functools.partial(kernel, rows), out_shape=jax.ShapeDtypeS...  16.4 us
    unnamed x1, local copies, waits for them, and re-layouts  0.66 us

profile of v5, /device:TPU:449, one launch (start us, length us, event | category | flops | bytes accessed | tf_op | source)
XLA Modules:
  0.0 17.7 jit_solution(8198372981414762141)
XLA Ops:
  0.7 16.4 %correlate.1 = f32[16,2048]{1,0:T(8,128)S(1)} custom-call(f32[1024,128]{1,0:T(8,128)} %bitcast.2, s32[2,32]{1,0:T(2,128)} %bitcast.3, s32[1]{0:T(128)S(6)} %copy.8.live_pairs, bf16[2,256,256]{2,1,0:T(8,128)(2,1)} %constant.6.clone.forward_hbm, bf16[2,256,256]{2,1,0:T(8,128)(2,1)} %constant.7.clone.inverse_hbm, f32[56,128]{1,0:T(8,128)} %constant.8.clone.small_hbm), custom_call_target="tpu_custom_call" | custom-call | tf_op jit(solution)/shard_map/correlate/pallas_call | solution.py:383
  17.0 0.7 %copy.9 = f32[16,2048]{1,0:T(8,128)} copy(f32[16,2048]{1,0:T(8,128)S(1)} %correlate.1) | data formatting | bytes 262144

commit v6 on v5

--- a/solution.py
+++ b/solution.py
@@ -118,8 +118,8 @@
 
 
 def spectra(x_ref, small, forward, base):
-    first = pl.multiple_of(base * RADIX, CHUNK * RADIX)
-    values = [x_ref[pl.ds(first + n1, CHUNK, stride=RADIX), :] for n1 in range(RADIX)]
+    first = pl.multiple_of(base * PITCH, CHUNK * PITCH)
+    values = [x_ref[pl.ds(first + n1, CHUNK, stride=PITCH), :] for n1 in range(RADIX)]
     turned_re, turned_im = [], []
     for s, (re, im) in enumerate(real_dft(values)):
         c, n = small[s : s + 1, :], small[17 + s : 18 + s, :]
@@ -213,9 +213,17 @@
     kept = rows // 2
     ext = (ext_0, ext_1)
 
-    def load(i):
-        place = (pl.ds(0, CHUNK * RADIX), pl.ds(CHUNK * RADIX, (rows - CHUNK) * RADIX))[i]
-        return pltpu.make_async_copy(traces.at[place], x_ref.at[place], load_sem.at[i])
+    def load(channel):
+        return pltpu.make_async_copy(
+            traces.at[pl.ds(channel * RADIX, RADIX)],
+            x_ref.at[pl.ds(channel * PITCH, RADIX)],
+            load_sem.at[0 if channel < CHUNK else 1],
+        )
+
+    def loaded(i):
+        size = CHUNK * RADIX if i == 0 else (rows - CHUNK) * RADIX
+        place = x_ref.at[pl.ds(0, size)]
+        return pltpu.make_async_copy(traces.at[pl.ds(0, size)], place, load_sem.at[i])
 
     table_loads = [
         pltpu.make_async_copy(src, dst, table_sem.at[i])
@@ -233,49 +241,62 @@
     last = (me == count - 1).astype(jnp.int32)
     other = 1 - core
     ways = (
-        ((me - 1 + first, core + first * (other - core)), 2 * rows * (1 - first), first),
-        ((me + 1 - last, core + last * (other - core)), 2 * rows * last, 1 - last),
+        ((me - 1 + first, core + first * (other - core)), 2 * rows * (1 - first)),
+        ((me + 1 - last, core + last * (other - core)), 2 * rows * last),
     )
     barrier = pltpu.get_barrier_semaphore()
     for target in (ways[0][0], ways[1][0], (me, other)):
         pl.semaphore_signal(barrier, inc=1, device_id=target, device_id_type=MESH)
 
-    load(0).start()
+    for channel in range(CHUNK):
+        load(channel).start()
     table_loads[0].start()
     table_loads[1].start()
-    load(1).start()
+    for channel in range(CHUNK, rows):
+        load(channel).start()
     for copy in table_loads[2:]:
         copy.start()
 
     def send(way, half, start, size):
-        target, place, side = ways[way]
+        target, place = ways[way]
         return pltpu.make_async_remote_copy(
             src_ref=ext[half].at[pl.ds(rows + start, size)],
             dst_ref=ext[half].at[pl.ds(place + start, size)],
-            send_sem=send_sem.at[way, half],
-            recv_sem=recv_sem.at[side, half],
+            send_sem=send_sem.at[way],
+            recv_sem=recv_sem.at[half],
             device_id=target,
             device_id_type=MESH,
         )
 
-    def arrival(side, half):
-        place = ext[half].at[pl.ds((1 - side) * 2 * rows, rows)]
+    def sent(way):
+        place = ext_0.at[pl.ds(0, 2 * rows)]
         return pltpu.make_async_remote_copy(
             src_ref=place,
             dst_ref=place,
-            send_sem=send_sem.at[0, half],
-            recv_sem=recv_sem.at[side, half],
+            send_sem=send_sem.at[way],
+            recv_sem=recv_sem.at[0],
             device_id=(me, other),
             device_id_type=MESH,
         )
 
-    load(0).wait()
+    def arrivals(half):
+        place = ext[half].at[pl.ds(0, 2 * rows)]
+        return pltpu.make_async_remote_copy(
+            src_ref=place,
+            dst_ref=place,
+            send_sem=send_sem.at[0],
+            recv_sem=recv_sem.at[half],
+            device_id=(me, other),
+            device_id_type=MESH,
+        )
+
+    loaded(0).wait()
     table_loads[0].wait()
     table_loads[1].wait()
 
     def transform(i, carry):
         start = pl.multiple_of(i * CHUNK, CHUNK)
-        pl.when(i == 1)(load(1).wait)
+        pl.when(i == 1)(loaded(1).wait)
         re, im = spectra(x_ref, small, forward, start)
         for s, (a, b) in enumerate(whitened(re, im, small)):
             place = s // 8 * 16 + s % 8
@@ -322,8 +343,7 @@
         )
 
     for half in range(2):
-        for side in range(2):
-            arrival(side, half).wait_recv()
+        arrivals(half).wait_recv()
         for i in range(kept):
             cross(half, cross_out, other * kept + i, i)
         swap(half).start()
@@ -368,8 +388,7 @@
                 wanted, blocks[l1 % RADIX], 0.0
             )
     for way in range(2):
-        for half in range(2):
-            send(way, half, 0, rows).wait_send()
+        sent(way).wait_send()
 
 
 def shards(traces, pair_list, live_pairs):
@@ -388,7 +407,7 @@
         scratch_shapes=[
             pltpu.SMEM((2, rows), jnp.int32),
             pltpu.SMEM((1,), jnp.int32),
-            pltpu.VMEM((rows * RADIX, LANES), f32),
+            pltpu.VMEM((rows * PITCH, LANES), f32),
             pltpu.VMEM(forward.shape, bf16),
             pltpu.VMEM(inverse.shape, bf16),
             pltpu.VMEM(small.shape, f32),
@@ -400,8 +419,8 @@
             pltpu.VMEM((2, 2, 8 * kept, LANES), f32),
             pltpu.SemaphoreType.DMA((2,)),
             pltpu.SemaphoreType.DMA((5,)),
-            pltpu.SemaphoreType.DMA((2, 2)),
-            pltpu.SemaphoreType.DMA((2, 2)),
+            pltpu.SemaphoreType.DMA((2,)),
+            pltpu.SemaphoreType.DMA((2,)),
             pltpu.SemaphoreType.DMA((2, 2)),
         ],
         compiler_params=pltpu.CompilerParams(

time: 17.8 us -> 17.9 us (level)
  no operation moved by 1% of the time
where the time goes in v6:
time: 17.9 us; the launch traced here: 17.7 us
  Pallas kernels  16.4 us (92%)
  local copies, waits for them, and re-layouts  0.66 us (4%)
  between operations  0.66 us (4%)
    pallas_call x1, Pallas kernels, shards(): pl.pallas_call(functools.partial(kernel, rows), out_shape=jax.ShapeDtypeS...  16.4 us
    unnamed x1, local copies, waits for them, and re-layouts  0.66 us

profile of v6, /device:TPU:449, one launch (start us, length us, event | category | flops | bytes accessed | tf_op | source)
XLA Modules:
  0.0 17.7 jit_solution(15213486037252663853)
XLA Ops:
  0.7 16.4 %correlate.1 = f32[16,2048]{1,0:T(8,128)S(1)} custom-call(f32[1024,128]{1,0:T(8,128)} %bitcast.2, s32[2,32]{1,0:T(2,128)} %bitcast.3, s32[1]{0:T(128)S(6)} %copy.8.live_pairs, bf16[2,256,256]{2,1,0:T(8,128)(2,1)} %constant.6.clone.forward_hbm, bf16[2,256,256]{2,1,0:T(8,128)(2,1)} %constant.7.clone.inverse_hbm, f32[56,128]{1,0:T(8,128)} %constant.8.clone.small_hbm), custom_call_target="tpu_custom_call" | custom-call | tf_op jit(solution)/shard_map/correlate/pallas_call | solution.py:402
  17.1 0.7 %copy.9 = f32[16,2048]{1,0:T(8,128)} copy(f32[16,2048]{1,0:T(8,128)S(1)} %correlate.1) | data formatting | bytes 262144

commit v7 on v6

--- a/solution.py
+++ b/solution.py
@@ -189,6 +189,7 @@
     small_hbm,
     out_ref,
     members,
+    local,
     live,
     x_ref,
     forward,
@@ -244,14 +245,14 @@
         ((me - 1 + first, core + first * (other - core)), 2 * rows * (1 - first)),
         ((me + 1 - last, core + last * (other - core)), 2 * rows * last),
     )
-    barrier = pltpu.get_barrier_semaphore()
-    for target in (ways[0][0], ways[1][0], (me, other)):
-        pl.semaphore_signal(barrier, inc=1, device_id=target, device_id_type=MESH)
-
     for channel in range(CHUNK):
         load(channel).start()
     table_loads[0].start()
     table_loads[1].start()
+    barrier = pltpu.get_barrier_semaphore()
+    for target in (ways[0][0], ways[1][0], (me, other)):
+        pl.semaphore_signal(barrier, inc=1, device_id=target, device_id_type=MESH)
+
     for channel in range(CHUNK, rows):
         load(channel).start()
     for copy in table_loads[2:]:
@@ -322,9 +323,15 @@
     table_loads[4].wait()
     anchor = me * rows - rows
 
+    def localise(slot, carry):
+        for k in range(2):
+            local[k, slot] = jnp.clip(members[k, slot] - anchor, 0, 3 * rows - 1)
+        return carry
+
+    lax.fori_loop(0, rows, localise, 0)
+
     def cross(half, into, slot, i):
-        one = jnp.clip(members[0, slot] - anchor, 0, 3 * rows - 1)
-        two = jnp.clip(members[1, slot] - anchor, 0, 3 * rows - 1)
+        one, two = local[0, slot], local[1, slot]
         a = ext[half][one].astype(jnp.float32)
         b = ext[half][two].astype(jnp.float32)
         ar, ai, br, bi = a[:8], a[8:], b[:8], b[8:]
@@ -406,6 +413,7 @@
         out_specs=pl.BlockSpec(memory_space=pltpu.VMEM),
         scratch_shapes=[
             pltpu.SMEM((2, rows), jnp.int32),
+            pltpu.SMEM((2, rows), jnp.int32),
             pltpu.SMEM((1,), jnp.int32),
             pltpu.VMEM((rows * PITCH, LANES), f32),
             pltpu.VMEM(forward.shape, bf16),

time: 17.9 us -> 17.7 us (0.989)
  Pallas kernels: 16.4 us -> 16.2 us
where the time goes in v7:
time: 17.7 us; the launch traced here: 17.5 us
  Pallas kernels  16.2 us (92%)
  local copies, waits for them, and re-layouts  0.66 us (4%)
  between operations  0.66 us (4%)
    pallas_call x1, Pallas kernels, shards(): pl.pallas_call(functools.partial(kernel, rows), out_shape=jax.ShapeDtypeS...  16.2 us
    unnamed x1, local copies, waits for them, and re-layouts  0.66 us

profile of v7, /device:TPU:449, one launch (start us, length us, event | category | flops | bytes accessed | tf_op | source)
XLA Modules:
  0.0 17.5 jit_solution(12619847773972284283)
XLA Ops:
  0.7 16.2 %correlate.1 = f32[16,2048]{1,0:T(8,128)S(1)} custom-call(f32[1024,128]{1,0:T(8,128)} %bitcast.2, s32[2,32]{1,0:T(2,128)} %bitcast.3, s32[1]{0:T(128)S(6)} %copy.8.live_pairs, bf16[2,256,256]{2,1,0:T(8,128)(2,1)} %constant.6.clone.forward_hbm, bf16[2,256,256]{2,1,0:T(8,128)(2,1)} %constant.7.clone.inverse_hbm, f32[56,128]{1,0:T(8,128)} %constant.8.clone.small_hbm), custom_call_target="tpu_custom_call" | custom-call | tf_op jit(solution)/shard_map/correlate/pallas_call | solution.py:409
  16.9 0.7 %copy.9 = f32[16,2048]{1,0:T(8,128)} copy(f32[16,2048]{1,0:T(8,128)S(1)} %correlate.1) | data formatting | bytes 262144

commit v8 on v7

--- a/solution.py
+++ b/solution.py
@@ -114,7 +114,8 @@
 def dot3(value, table):
     high, low = halves(value)
     dot = functools.partial(jnp.dot, preferred_element_type=jnp.float32)
-    return dot(high, table[0]) + (dot(low, table[0]) + dot(high, table[1]))
+    depth = jnp.concatenate([table[0], table[1]], axis=0)
+    return dot(jnp.concatenate([high, high], axis=1), depth) + dot(low, table[0])
 
 
 def spectra(x_ref, small, forward, base):
@@ -255,8 +256,6 @@
 
     for channel in range(CHUNK, rows):
         load(channel).start()
-    for copy in table_loads[2:]:
-        copy.start()
 
     def send(way, half, start, size):
         target, place = ways[way]
@@ -294,6 +293,8 @@
     loaded(0).wait()
     table_loads[0].wait()
     table_loads[1].wait()
+    for copy in table_loads[2:]:
+        copy.start()
 
     def transform(i, carry):
         start = pl.multiple_of(i * CHUNK, CHUNK)

time: 17.7 us -> 17.7 us (level)
  no operation moved by 1% of the time
where the time goes in v8:
time: 17.7 us; the launch traced here: 17.5 us
  Pallas kernels  16.2 us (92%)
  local copies, waits for them, and re-layouts  0.66 us (4%)
  between operations  0.66 us (4%)
    pallas_call x1, Pallas kernels, shards(): pl.pallas_call(functools.partial(kernel, rows), out_shape=jax.ShapeDtypeS...  16.2 us
    unnamed x1, local copies, waits for them, and re-layouts  0.66 us

profile of v8, /device:TPU:449, one launch (start us, length us, event | category | flops | bytes accessed | tf_op | source)
XLA Modules:
  0.0 17.5 jit_solution(4814239178962464868)
XLA Ops:
  0.7 16.2 %correlate.1 = f32[16,2048]{1,0:T(8,128)S(1)} custom-call(f32[1024,128]{1,0:T(8,128)} %bitcast.2, s32[2,32]{1,0:T(2,128)} %bitcast.3, s32[1]{0:T(128)S(6)} %copy.8.live_pairs, bf16[2,256,256]{2,1,0:T(8,128)(2,1)} %constant.6.clone.forward_hbm, bf16[2,256,256]{2,1,0:T(8,128)(2,1)} %constant.7.clone.inverse_hbm, f32[56,128]{1,0:T(8,128)} %constant.8.clone.small_hbm), custom_call_target="tpu_custom_call" | custom-call | tf_op jit(solution)/shard_map/correlate/pallas_call | solution.py:410
  16.9 0.7 %copy.9 = f32[16,2048]{1,0:T(8,128)} copy(f32[16,2048]{1,0:T(8,128)S(1)} %correlate.1) | data formatting | bytes 262144

commit v9 on v8

--- a/solution.py
+++ b/solution.py
@@ -114,8 +114,7 @@
 def dot3(value, table):
     high, low = halves(value)
     dot = functools.partial(jnp.dot, preferred_element_type=jnp.float32)
-    depth = jnp.concatenate([table[0], table[1]], axis=0)
-    return dot(jnp.concatenate([high, high], axis=1), depth) + dot(low, table[0])
+    return dot(high, table[0]) + (dot(low, table[0]) + dot(high, table[1]))
 
 
 def spectra(x_ref, small, forward, base):

time: 17.7 us -> 17.7 us (level)
  no operation moved by 1% of the time
where the time goes in v9:
time: 17.7 us; the launch traced here: 17.5 us
  Pallas kernels  16.2 us (92%)
  local copies, waits for them, and re-layouts  0.66 us (4%)
  between operations  0.66 us (4%)
    pallas_call x1, Pallas kernels, shards(): pl.pallas_call(functools.partial(kernel, rows), out_shape=jax.ShapeDtypeS...  16.2 us
    unnamed x1, local copies, waits for them, and re-layouts  0.66 us

profile of v9, /device:TPU:449, one launch (start us, length us, event | category | flops | bytes accessed | tf_op | source)
XLA Modules:
  0.0 17.5 jit_solution(11345178219234378539)
XLA Ops:
  0.7 16.2 %correlate.1 = f32[16,2048]{1,0:T(8,128)S(1)} custom-call(f32[1024,128]{1,0:T(8,128)} %bitcast.2, s32[2,32]{1,0:T(2,128)} %bitcast.3, s32[1]{0:T(128)S(6)} %copy.8.live_pairs, bf16[2,256,256]{2,1,0:T(8,128)(2,1)} %constant.6.clone.forward_hbm, bf16[2,256,256]{2,1,0:T(8,128)(2,1)} %constant.7.clone.inverse_hbm, f32[56,128]{1,0:T(8,128)} %constant.8.clone.small_hbm), custom_call_target="tpu_custom_call" | custom-call | tf_op jit(solution)/shard_map/correlate/pallas_call | solution.py:409
  16.9 0.7 %copy.9 = f32[16,2048]{1,0:T(8,128)} copy(f32[16,2048]{1,0:T(8,128)S(1)} %correlate.1) | data formatting | bytes 262144
